TPU v7x, 128 devices: a whole 4x4x4 slice. The times are simulated.
128 devices in a mesh: dp: 4 (over y), tm: 4 (over z), height: 8 (over x, core).
Axes of the slice: x: 4, y: 4, z: 4, core: 2. Of those that a mesh axis runs over, the one named last changes fastest.
Arguments:
- latents: bfloat16 [4, 8, 32, 160, 128], P('dp', 'tm', 'height'), may hold values from -40 to 40
- cotangent: bfloat16 [4, 8, 64, 320, 128], P('dp', 'tm', 'height'), may hold values from -6 to 6
- group_norm_gain: float32 [128], replicated, may hold values from 0.5 to 1.5
- group_norm_bias: float32 [128], replicated, may hold values from -3 to 3
- kernel: bfloat16 [3, 3, 384, 128], replicated, may hold values from -0.109375 to 0.109375
- kernel_bias: float32 [128], replicated, may hold values from -3 to 3
Outputs:
- upsampled: bfloat16 [4, 8, 64, 320, 128], P('dp', 'tm', 'height')
- latent_gradient: bfloat16 [4, 8, 32, 160, 128], P('dp', 'tm', 'height')
- kernel_grad: float32 [3, 3, 384, 128], replicated
- bias_grad: float32 [128], replicated
- gain_grad: float32 [128], replicated
- shift_grad: float32 [128], replicated
All inputs are finite; a program needn't handle non-finite values.
Results may differ from a plain program's by a relative error of at most 0.0051.
Values may be sent and summed in bfloat16 or wider, within the bound.
A program may use at most 128 MiB of HBM per device.

v0:
```python
import functools

import jax
import jax.numpy as jnp
from jax import lax
from jax.experimental import pallas as pl
from jax.experimental.pallas import tpu as pltpu
from jax.sharding import PartitionSpec as P

MESH = pl.DeviceIdType.MESH
GROUPS = 32
F32 = jnp.float32
BF16 = jnp.bfloat16

ORDER = {2: ("x", "y", "z"), 1: ("y", "z", "x"), 0: ("z", "x", "y")}


def body(
    count,
    lat_hbm,
    cot_hbm,
    gain_ref,
    bias_ref,
    ker_hbm,
    kbias_ref,
    up_hbm,
    lg_hbm,
    kg_hbm,
    small_ref,
    lat,
    cot,
    ker,
    kt,
    dc,
    dslab,
    aslab,
    line,
    pool,
    xhat_s,
    dsilu_s,
    act_s,
    actt,
    acc,
    up,
    lg,
    kg,
    g,
    rc,
    s1,
    r1,
    e2,
    e3,
    fin,
    st1,
    st2,
    gr1,
    gr2,
    gr3,
    lsem,
    osem,
    lat_ss,
    lat_rs,
    dc_ss,
    dc_rs,
    sm_ss,
    sm_rs,
    ar_ss,
    ar_rs,
):
    y = lax.axis_index("dp")
    z = lax.axis_index("tm")
    h = lax.axis_index("height")
    x = lax.div(h, 2)
    core = lax.rem(h, 2)
    first, last = z == 0, z == 3
    has_prev, has_next = z > 0, z < 3
    top, bottom = h == 0, h == 7
    has_up, has_down = h > 0, h < 7

    def peer(axis, d):
        if axis == "x":
            return {"height": 2 * lax.rem(x + d, 4) + core}
        if axis == "y":
            return {"dp": lax.rem(y + d, 4)}
        if axis == "z":
            return {"tm": lax.rem(z + d, 4)}
        if axis == "h":
            return {"height": lax.rem(h + d, 8)}
        return {"height": 2 * x + 1 - core}

    place = {"x": x, "y": y, "z": z, "h": h}
    size = {"x": 4, "y": 4, "z": 4, "h": 8}

    def remote(src, dst, ss, rs, to):
        return pltpu.make_async_remote_copy(
            src_ref=src, dst_ref=dst, send_sem=ss, recv_sem=rs, device_id=to, device_id_type=MESH
        )

    barrier = pltpu.get_barrier_semaphore()
    greeted = [peer("h", d) for d in range(1, 8)]
    greeted += [peer("z", d) for d in range(1, 4)] + [peer("y", d) for d in range(1, 4)]
    for to in greeted:
        pl.semaphore_signal(barrier, inc=1, device_id=to, device_id_type=MESH)

    loads = [
        pltpu.make_async_copy(cot_hbm.at[0, 0], cot.at[0], lsem.at[0]),
        pltpu.make_async_copy(lat_hbm.at[0], lat.at[2:4, 1:5], lsem.at[1]),
        pltpu.make_async_copy(cot_hbm.at[0, 1], cot.at[1], lsem.at[2]),
        pltpu.make_async_copy(ker_hbm, ker, lsem.at[3]),
    ]
    for c in loads:
        c.start()

    row16 = lax.broadcasted_iota(jnp.int32, (16, 128), 0)

    def grad_line(slot, r, v):
        line[8:168, :] = v
        line[7:8, :] = jnp.zeros((1, 128), F32)
        line[168:169, :] = jnp.zeros((1, 128), F32)
        dslab[slot, r, :, 128:256] = v.astype(BF16)
        dslab[slot, r, 16:160, 0:128] = line[25:169, :].astype(BF16)
        dslab[slot, r, 0:16, 0:128] = (
            line[9:25, :] + jnp.where(row16 == 0, v[0:16], 0.0)
        ).astype(BF16)
        dslab[slot, r, 0:144, 256:384] = line[7:151, :].astype(BF16)
        dslab[slot, r, 144:160, 256:384] = (
            line[151:167, :] + jnp.where(row16 == 15, v[144:160], 0.0)
        ).astype(BF16)

    def pool_frame(t, total):
        def step(r, total):
            a = cot[t, 2 * r].astype(F32) + cot[t, 2 * r + 1].astype(F32)
            pool[...] = a
            v32 = pool[pl.ds(0, 160, stride=2), :] + pool[pl.ds(1, 160, stride=2), :]
            total = total + v32.reshape(20, 8, 128).sum(axis=0)
            v = v32.astype(BF16)
            dc[t, r + 1] = v
            grad_line(3 * t, r + 1, v.astype(F32))
            return total

        return lax.fori_loop(0, 4, step, total)

    loads[0].wait()
    bias_total = pool_frame(0, jnp.zeros((8, 128), F32))
    loads[2].wait()
    bias_total = pool_frame(1, bias_total)

    loads[1].wait()

    def stat_step(n, carry):
        s, q = carry
        v = lat[2 + n // 4, 1 + n % 4].astype(F32).reshape(20, 8, 128)
        return s + v.sum(axis=0), q + (v * v).sum(axis=0)

    zero8 = jnp.zeros((8, 128), F32)
    s_sum, q_sum = lax.fori_loop(0, 8, stat_step, (zero8, zero8))
    row8 = lax.broadcasted_iota(jnp.int32, (8, 128), 0)

    def rows_of(*vectors):
        out = zero8
        for n, v in enumerate(vectors):
            out = jnp.where(row8 == n, v.sum(axis=0, keepdims=True), out)
        return out

    st1[h] = rows_of(s_sum, q_sum)

    pl.semaphore_wait(barrier, 13)

    def exchange_start(buf, axis, base):
        me = place[axis]
        out = []
        for d in range(1, size[axis]):
            c = remote(
                buf.at[me], buf.at[me], sm_ss.at[base + d], sm_rs.at[base + d], peer(axis, d)
            )
            c.start()
            out.append(c)
        return out

    def exchange_wait(copies):
        for c in copies:
            c.wait_recv()

    def tile_sum(buf, axis):
        out = buf[0]
        for n in range(1, size[axis]):
            out = out + buf[n]
        return out

    def dc_z(t, part):
        rows = (slice(1, 2), slice(4, 5), slice(2, 4))[part]
        n = 3 * t + part
        return remote(
            dc.at[t, rows],
            dc.at[2 + t, rows],
            dc_ss.at[n],
            dc_rs.at[n],
            {"tm": jnp.maximum(z - 1, 0)},
        )

    def dc_row(f, down):
        n = 6 + 2 * f + down
        src, dst = (4, 0) if down else (1, 5)
        to = {"height": jnp.minimum(h + 1, 7) if down else jnp.maximum(h - 1, 0)}
        return remote(dc.at[f, src], dc.at[f, dst], dc_ss.at[n], dc_rs.at[n], to)

    def lat_z(part):
        rows = (slice(1, 2), slice(4, 5), slice(2, 4))[part]
        return remote(
            lat.at[2:4, rows],
            lat.at[0:2, rows],
            lat_ss.at[part],
            lat_rs.at[part],
            {"tm": jnp.minimum(z + 1, 3)},
        )

    def lat_row(base, down):
        n = 3 + base + down
        src, dst = (4, 0) if down else (1, 5)
        to = {"height": jnp.minimum(h + 1, 7) if down else jnp.maximum(h - 1, 0)}
        return remote(
            lat.at[base : base + 2, src],
            lat.at[base : base + 2, dst],
            lat_ss.at[n],
            lat_rs.at[n],
            to,
        )

    stat_h = exchange_start(st1, "h", 0)

    @pl.when(has_prev)
    def _():
        for t in range(2):
            for part in range(3):
                dc_z(t, part).start()

    @pl.when(has_up)
    def _():
        dc_row(0, 0).start()
        dc_row(1, 0).start()
        lat_row(2, 0).start()

    @pl.when(has_down)
    def _():
        dc_row(0, 1).start()
        dc_row(1, 1).start()
        lat_row(2, 1).start()

    @pl.when(has_next)
    def _():
        for part in range(3):
            lat_z(part).start()

    exchange_wait(stat_h)
    st2[z] = tile_sum(st1, "h")
    stat_z = exchange_start(st2, "z", 8)

    loads[3].wait()

    def flip(n, carry):
        i, j = n // 3, n % 3
        for k in range(3):
            kt[i, pl.ds(pl.multiple_of(j * 384 + k * 128, 128), 128), :] = ker[
                i, j, k * 128 : (k + 1) * 128, :
            ].T
        return carry

    lax.fori_loop(0, 9, flip, 0)

    @pl.when(top)
    def _():
        for f in range(4):
            dc[f, 0] = jnp.zeros((160, 128), BF16)

    @pl.when(bottom)
    def _():
        for f in range(4):
            dc[f, 5] = jnp.zeros((160, 128), BF16)

    @pl.when(has_up)
    def _():
        dc_row(0, 1).wait_recv()
        dc_row(1, 1).wait_recv()

    @pl.when(has_down)
    def _():
        dc_row(0, 0).wait_recv()
        dc_row(1, 0).wait_recv()

    def grad_row(slot, f, r):
        grad_line(slot, r, dc[f, r].astype(F32))

    def edge_rows(n, carry):
        grad_row(3 * (n // 2), n // 2, 5 * (n % 2))
        return carry

    lax.fori_loop(0, 4, edge_rows, 0)

    def special_rows(slot):
        @pl.when(top)
        def _():
            dslab[slot, 6] = dslab[slot, 2] + dslab[slot, 1]

        @pl.when(bottom)
        def _():
            dslab[slot, 7] = dslab[slot, 3] + dslab[slot, 4]

    special_rows(0)
    special_rows(3)

    @pl.when(first)
    def _():
        def add(r, carry):
            dslab[1, r] = dslab[0, r] + dslab[3, r]
            return carry

        lax.fori_loop(0, 6, add, 0)
        special_rows(1)

    row_t = jnp.where(top, 6, 2)
    row_b = jnp.where(bottom, 7, 3)

    def taken(slot, j):
        if j == 0:
            parts = [dslab[pl.ds(slot, 1), pl.ds(row_t, 1)][0], dslab[slot, 3:6]]
        elif j == 1:
            parts = [dslab[slot, 1:5]]
        else:
            parts = [dslab[slot, 0:3], dslab[pl.ds(slot, 1), pl.ds(row_b, 1)][0]]
        v = jnp.concatenate(parts, axis=0) if len(parts) > 1 else parts[0]
        return v.reshape(640, 384)

    slot_of = {
        (0, 2): 0,
        (0, 1): jnp.where(first, 1, 3),
        (0, 0): jnp.where(first, 2, 4),
        (1, 2): 3,
        (1, 1): 4,
        (1, 0): 5,
    }

    exchange_wait(stat_z)
    lane_a = lax.broadcasted_iota(jnp.int32, (128, 128), 0) >> 2
    lane_b = lax.broadcasted_iota(jnp.int32, (128, 128), 1) >> 2
    same = jnp.where(lane_a == lane_b, 1.0, 0.0)

    def by_group(v):
        return jnp.dot(v, same, precision=lax.Precision.HIGHEST, preferred_element_type=F32)

    sums = by_group(tile_sum(st2, "z")) / count
    mean = sums[0:1]
    rstd = lax.rsqrt(sums[1:2] - mean * mean + 1e-6)
    gain = gain_ref[...]
    shift = bias_ref[...]

    def act_row(f, r, own):
        v = (lat[f, r].astype(F32) - mean) * rstd
        pre = v * gain + shift
        sig = 1.0 / (1.0 + jnp.exp(-pre))
        a = pre * sig
        if own:
            n = (f - 2) * 4 + r - 1
            rows = pl.ds(pl.multiple_of(n * 160, 160), 160)
            xhat_s[rows, :] = v
            dsilu_s[rows, :] = sig * (1.0 + pre * (1.0 - sig))
            act_s[rows, :] = a
        line[8:168, :] = a
        line[7:8, :] = a[0:1]
        line[168:169, :] = a[159:160]
        aslab[f, r, :, 0:128] = line[7:167, :].astype(BF16)
        aslab[f, r, :, 128:256] = a.astype(BF16)
        aslab[f, r, :, 256:384] = line[9:169, :].astype(BF16)

    def own_rows(n, carry):
        act_row(2 + n // 4, 1 + n % 4, True)
        return carry

    lax.fori_loop(0, 8, own_rows, 0)

    def transposed(n, carry):
        rows = pl.ds(pl.multiple_of(n * 128, 128), 128)
        actt[:, rows] = act_s[rows, :].T.astype(BF16)
        return carry

    lax.fori_loop(0, 10, transposed, 0)

    def weight_grad(i):
        for j in range(3):
            right = jnp.concatenate([taken(slot_of[0, i], j), taken(slot_of[1, i], j)], axis=0)
            part = jnp.dot(actt[...], right, preferred_element_type=F32)
            g[i, :, :, j * 384 : (j + 1) * 384] = part.astype(BF16).reshape(8, 16, 384)

    copies = {}

    def copy_c(i):
        c = remote(
            g.at[i, pl.ds((1 - core) * 4, 4)],
            rc.at[i],
            ar_ss.at[i, 0],
            ar_rs.at[i, 0],
            peer("core", 0),
        )
        c.start()
        copies[i, 0] = [c]

    def reduce_1(i):
        for c in copies[i, 0]:
            c.wait_recv()
        s1[i] = (g[i, pl.ds(core * 4, 4)].astype(F32) + rc[i].astype(F32)).astype(BF16)
        axis = ORDER[i][0]
        me = place[axis]
        copies[i, 1] = []
        for d in range(1, 4):
            c = remote(
                s1.at[i, lax.rem(me + d, 4)],
                r1.at[i, me],
                ar_ss.at[i, d],
                ar_rs.at[i, d],
                peer(axis, d),
            )
            c.start()
            copies[i, 1].append(c)
        r1[i, me] = s1[i, me]

    def exchange(i, step, buf):
        axis = ORDER[i][step - 1]
        me = place[axis]
        copies[i, step] = []
        for d in range(1, 4):
            n = 3 * (step - 1) + d
            c = remote(buf.at[i, me], buf.at[i, me], ar_ss.at[i, n], ar_rs.at[i, n], peer(axis, d))
            c.start()
            copies[i, step].append(c)

    def total_of(buf, i):
        out = buf[i, 0].astype(F32)
        for n in range(1, 4):
            out = out + buf[i, n].astype(F32)
        return out.astype(BF16)

    def reduce_2(i):
        for c in copies[i, 1]:
            c.wait_recv()
        e2[i, place[ORDER[i][1]]] = total_of(r1, i)
        exchange(i, 2, e2)

    def reduce_3(i):
        for c in copies[i, 2]:
            c.wait_recv()
        e3[i, place[ORDER[i][2]]] = total_of(e2, i)
        exchange(i, 3, e3)

    def gather_1(i):
        for c in copies[i, 3]:
            c.wait_recv()
        axis = ORDER[i][0]
        me = core * 4 + place[axis]
        fin[i, me] = total_of(e3, i)
        copies[i, 4] = []
        for d in range(1, 4):
            n = 9 + d
            c = remote(fin.at[i, me], fin.at[i, me], ar_ss.at[i, n], ar_rs.at[i, n], peer(axis, d))
            c.start()
            copies[i, 4].append(c)

    def gather_c(i):
        for c in copies[i, 4]:
            c.wait_recv()
        half = pl.ds(core * 4, 4)
        c = remote(
            fin.at[i, half], fin.at[i, half], ar_ss.at[i, 13], ar_rs.at[i, 13], peer("core", 0)
        )
        c.start()
        copies[i, 5] = [c]

    outs = []

    def finish(i):
        for c in copies[i, 5]:
            c.wait_recv()
        for n in range(9):
            j, k = divmod(n, 3)
            kg[i, j, k * 128 : (k + 1) * 128, :] = (
                fin[i, :, :, n * 128 : (n + 1) * 128].reshape(128, 128).astype(F32)
            )
        c = pltpu.make_async_copy(kg.at[i], kg_hbm.at[i], osem.at[i])
        c.start()
        outs.append(c)

    weight_grad(2)
    copy_c(2)

    @pl.when(last)
    def _():
        for f in range(2, 4):
            for r in range(6):
                dc[f, r] = jnp.zeros((160, 128), BF16)

    def ahead(t):
        f = 2 + t

        @pl.when(has_next)
        def _():
            dc_z(t, 0).wait_recv()
            dc_z(t, 1).wait_recv()

            @pl.when(has_up)
            def _():
                dc_row(f, 0).start()

            @pl.when(has_down)
            def _():
                dc_row(f, 1).start()

            dc_z(t, 2).wait_recv()

        def inner(r, carry):
            grad_row(4 + t, f, r)
            return carry

        lax.fori_loop(1, 5, inner, 0)

        @pl.when(has_next)
        def _():
            @pl.when(has_up)
            def _():
                dc_row(f, 1).wait_recv()

            @pl.when(has_down)
            def _():
                dc_row(f, 0).wait_recv()

        def outer(n, carry):
            grad_row(4 + t, f, 5 * n)
            return carry

        lax.fori_loop(0, 2, outer, 0)
        special_rows(4 + t)

    ahead(0)

    @pl.when(first)
    def _():
        def add(r, carry):
            dslab[2, r] = dslab[1, r] + dslab[4, r]
            return carry

        lax.fori_loop(0, 6, add, 0)
        special_rows(2)

    reduce_1(2)
    weight_grad(1)
    copy_c(1)
    ahead(1)
    reduce_2(2)
    reduce_1(1)
    weight_grad(0)
    copy_c(0)

    def data_grad(p):
        rows = slice(p * 640, (p + 1) * 640)
        for i in (2, 1, 0):
            left = jnp.concatenate([taken(slot_of[p, i], j) for j in range(3)], axis=1)
            part = lax.dot_general(
                left, kt[i], (((1,), (0,)), ((), ())), preferred_element_type=F32
            )
            acc[rows, :] = part if i == 2 else acc[rows, :] + part

    data_grad(0)
    reduce_3(2)
    reduce_2(1)
    reduce_1(0)
    data_grad(1)

    def through(n, carry):
        a, b = carry
        rows = pl.ds(pl.multiple_of(n * 160, 160), 160)
        d = acc[rows, :] * dsilu_s[rows, :]
        acc[rows, :] = d
        b = b + (d * xhat_s[rows, :]).reshape(20, 8, 128).sum(axis=0)
        return a + d.reshape(20, 8, 128).sum(axis=0), b

    d_sum, dx_sum = lax.fori_loop(0, 8, through, (zero8, zero8))
    gr1[h] = rows_of(d_sum, dx_sum, bias_total)
    grad_h = exchange_start(gr1, "h", 12)
    gather_1(2)
    reduce_3(1)
    reduce_2(0)

    @pl.when(top)
    def _():
        for f in range(2, 4):
            lat[f, 0] = lat[f, 1]

    @pl.when(bottom)
    def _():
        for f in range(2, 4):
            lat[f, 5] = lat[f, 4]

    @pl.when(has_up)
    def _():
        lat_row(2, 1).wait_recv()

    @pl.when(has_down)
    def _():
        lat_row(2, 0).wait_recv()

    @pl.when(has_prev)
    def _():
        lat_z(0).wait_recv()
        lat_z(1).wait_recv()

        @pl.when(has_up)
        def _():
            lat_row(0, 0).start()

        @pl.when(has_down)
        def _():
            lat_row(0, 1).start()

        lat_z(2).wait_recv()

        @pl.when(top)
        def _():
            for f in range(2):
                lat[f, 0] = lat[f, 1]

        @pl.when(bottom)
        def _():
            for f in range(2):
                lat[f, 5] = lat[f, 4]

        @pl.when(has_up)
        def _():
            lat_row(0, 1).wait_recv()

        @pl.when(has_down)
        def _():
            lat_row(0, 0).wait_recv()

    @pl.when(first)
    def _():
        for f in range(2):
            for r in range(6):
                lat[f, r] = lat[2, r]

    exchange_wait(grad_h)
    gr2[z] = tile_sum(gr1, "h")
    grad_z = exchange_start(gr2, "z", 20)

    def edge_act(n, carry):
        act_row(2 + n // 2, 5 * (n % 2), False)
        return carry

    lax.fori_loop(0, 4, edge_act, 0)

    def past_act(n, carry):
        act_row(n // 6, n % 6, False)
        return carry

    lax.fori_loop(0, 12, past_act, 0)
    gather_c(2)
    gather_1(1)
    reduce_3(0)
    exchange_wait(grad_z)
    clip_sums = tile_sum(gr2, "z")
    gr3[y] = clip_sums
    grad_y = exchange_start(gr3, "y", 24)

    means = by_group(clip_sums * gain) / count
    mean_a, mean_b = means[0:1], means[1:2]

    def latent_grad(n, carry):
        rows = pl.ds(pl.multiple_of(n * 160, 160), 160)
        v = rstd * (acc[rows, :] * gain - mean_a - xhat_s[rows, :] * mean_b)
        lg[n // 4, n % 4] = v.astype(BF16)
        return carry

    lax.fori_loop(0, 8, latent_grad, 0)
    c = pltpu.make_async_copy(lg, lg_hbm.at[0], osem.at[3])
    c.start()
    outs.append(c)

    kbias = kbias_ref[...]

    def conv(t):
        rows = slice(t * 640, (t + 1) * 640)
        for i in range(3):
            left = jnp.concatenate(
                [aslab[t + i, j : j + 4].reshape(640, 384) for j in range(3)], axis=1
            )
            part = jnp.dot(left, ker[i].reshape(1152, 128), preferred_element_type=F32)
            act_s[rows, :] = part if i == 0 else act_s[rows, :] + part

        def expand(r, carry):
            v = act_s[pl.ds(pl.multiple_of((t * 4 + r) * 160, 160), 160), :] + kbias
            pool[pl.ds(0, 160, stride=2), :] = v
            pool[pl.ds(1, 160, stride=2), :] = v
            w = pool[...].astype(BF16)
            up[t, 2 * r] = w
            up[t, 2 * r + 1] = w
            return carry

        lax.fori_loop(0, 4, expand, 0)
        c = pltpu.make_async_copy(up.at[t], up_hbm.at[0, t], osem.at[4 + t])
        c.start()
        outs.append(c)

    conv(0)
    finish(2)
    gather_c(1)
    gather_1(0)
    conv(1)
    finish(1)
    gather_c(0)
    exchange_wait(grad_y)
    small_ref[...] = tile_sum(gr3, "y")
    finish(0)

    for group in (stat_h, stat_z, grad_h, grad_z, grad_y, *copies.values()):
        for c in group:
            c.wait_send()

    @pl.when(has_prev)
    def _():
        for t in range(2):
            for part in range(3):
                dc_z(t, part).wait_send()

    @pl.when(has_next)
    def _():
        for part in range(3):
            lat_z(part).wait_send()

    for down, there in ((0, has_up), (1, has_down)):

        @pl.when(there)
        def _(down=down):
            dc_row(0, down).wait_send()
            dc_row(1, down).wait_send()
            lat_row(2, down).wait_send()

            @pl.when(has_next)
            def _():
                dc_row(2, down).wait_send()
                dc_row(3, down).wait_send()

            @pl.when(has_prev)
            def _():
                lat_row(0, down).wait_send()

    for c in outs:
        c.wait()


def local(latents, cotangent, gain, bias, kernel, kernel_bias):
    count = 8 * 32 * 160 * (128 // GROUPS)
    hbm = pl.BlockSpec(memory_space=pl.ANY)
    vmem = pl.BlockSpec(memory_space=pltpu.VMEM)
    dma = pltpu.SemaphoreType.DMA
    up, lg, kg, small = pl.pallas_call(
        functools.partial(body, float(count)),
        out_shape=(
            jax.ShapeDtypeStruct((1, 2, 8, 320, 128), BF16),
            jax.ShapeDtypeStruct((1, 2, 4, 160, 128), BF16),
            jax.ShapeDtypeStruct((3, 3, 384, 128), F32),
            jax.ShapeDtypeStruct((8, 128), F32),
        ),
        in_specs=[hbm, hbm, vmem, vmem, hbm, vmem],
        out_specs=(hbm, hbm, hbm, vmem),
        scratch_shapes=[
            pltpu.VMEM((4, 6, 160, 128), BF16),
            pltpu.VMEM((2, 8, 320, 128), BF16),
            pltpu.VMEM((3, 3, 384, 128), BF16),
            pltpu.VMEM((3, 1152, 128), BF16),
            pltpu.VMEM((4, 6, 160, 128), BF16),
            pltpu.VMEM((6, 8, 160, 384), BF16),
            pltpu.VMEM((4, 6, 160, 384), BF16),
            pltpu.VMEM((176, 128), F32),
            pltpu.VMEM((320, 128), F32),
            pltpu.VMEM((1280, 128), F32),
            pltpu.VMEM((1280, 128), F32),
            pltpu.VMEM((1280, 128), F32),
            pltpu.VMEM((128, 1280), BF16),
            pltpu.VMEM((1280, 128), F32),
            pltpu.VMEM((2, 8, 320, 128), BF16),
            pltpu.VMEM((2, 4, 160, 128), BF16),
            pltpu.VMEM((3, 3, 384, 128), F32),
            pltpu.VMEM((3, 8, 16, 1152), BF16),
            pltpu.VMEM((3, 4, 16, 1152), BF16),
            pltpu.VMEM((3, 4, 16, 1152), BF16),
            pltpu.VMEM((3, 4, 16, 1152), BF16),
            pltpu.VMEM((3, 4, 16, 1152), BF16),
            pltpu.VMEM((3, 4, 16, 1152), BF16),
            pltpu.VMEM((3, 8, 16, 1152), BF16),
            pltpu.VMEM((8, 8, 128), F32),
            pltpu.VMEM((4, 8, 128), F32),
            pltpu.VMEM((8, 8, 128), F32),
            pltpu.VMEM((4, 8, 128), F32),
            pltpu.VMEM((4, 8, 128), F32),
            dma((4,)),
            dma((6,)),
            dma((7,)),
            dma((7,)),
            dma((14,)),
            dma((14,)),
            dma((28,)),
            dma((28,)),
            dma((3, 14)),
            dma((3, 14)),
        ],
        compiler_params=pltpu.CompilerParams(
            collective_id=0, has_side_effects=True, vmem_limit_bytes=50 * 1024 * 1024
        ),
        cost_estimate=pl.CostEstimate(flops=3 * 2 * 1280 * 3456 * 128, bytes_accessed=6000000, transcendentals=500000),
    )(latents, cotangent, gain[None], bias[None], kernel, kernel_bias[None])
    return up, lg, kg, small[2], small[1], small[0]


def solution(mesh):
    split = P("dp", "tm", "height", None, None)
    return jax.shard_map(
        local,
        mesh=mesh,
        in_specs=(split, split, P(), P(), P(), P()),
        out_specs=(split, split, P(), P(), P(), P()),
        check_vma=False,
    )
```

profile of v0, /device:TPU:1, one launch (start us, length us, event | category | flops | bytes accessed | tf_op | source)
XLA Modules:
  0.0 63.6 jit_solution(4064121314193120685)
XLA Ops:
  0.6 0.0 copy-start
  0.6 1.2 %copy-done = bf16[3,3,384,128]{3,2,1,0:T(8,128)(2,1)S(1)} copy-done((bf16[3,3,384,128]{3,2,1,0:T(8,128)(2,1)S(1)}, bf16[3,3,384,128]{3,2,1,0:T(8,128)(2,1)}, u32[]{:S(2)}) %copy-start) | copy-done | bytes 884760
  1.8 0.0 copy-start.1
  1.8 1.0 %copy-done.1 = bf16[1,2,4,160,128]{4,3,2,1,0:T(8,128)(2,1)S(1)} copy-done((bf16[1,2,4,160,128]{4,3,2,1,0:T(8,128)(2,1)S(1)}, bf16[1,2,4,160,128]{4,3,2,1,0:T(8,128)(2,1)}, u32[]{:S(2)}) %copy-start.1) | copy-done | bytes 327704
  2.8 0.0 copy-start.2
  2.8 0.7 %copy-done.2 = f32[128]{0:T(128)S(1)} copy-done((f32[128]{0:T(128)S(1)}, f32[128]{0:T(128)}, u32[]{:S(2)}) %copy-start.2) | copy-done | bytes 536
  3.4 0.0 copy-start.3
  3.4 0.7 %copy-done.3 = f32[128]{0:T(128)S(1)} copy-done((f32[128]{0:T(128)S(1)}, f32[128]{0:T(128)}, u32[]{:S(2)}) %copy-start.3) | copy-done | bytes 536
  4.1 0.0 copy-start.4
  4.1 0.7 %copy-done.4 = f32[128]{0:T(128)S(1)} copy-done((f32[128]{0:T(128)S(1)}, f32[128]{0:T(128)}, u32[]{:S(2)}) %copy-start.4) | copy-done | bytes 536
  4.7 55.2 %shard_map.109 = (bf16[1,2,8,320,128]{4,3,2,1,0:T(8,128)(2,1)S(1)}, bf16[1,2,4,160,128]{4,3,2,1,0:T(8,128)(2,1)S(1)}, f32[3,3,384,128]{3,2,1,0:T(8,128)}, f32[8,128]{1,0:T(8,128)S(1)}) custom-call(bf16[1,2,4,160,128]{4,3,2,1,0:T(8,128)(2,1)S(1)} %copy-done.1, bf16[1,2,8,320,128]{4,3,2,1,0:T(8,128)(2,1)} %cot_hbm.1, f32[1,128]{1,0:T(1,128)S(1)} %bitcast.9, ...), custom_call_target="tpu_custom_call" | custom-call | flops 3397386240 | bytes 6000000 | tf_op jit(solution)/shard_map/pallas_call | solution.py:761
  60.0 0.5 slice_bitcast_fusion
  60.5 0.0 copy-start.5
  60.5 1.1 %copy.15 = bf16[1,2,8,320,128]{4,3,2,1,0:T(8,128)(2,1)} copy(bf16[1,2,8,320,128]{4,3,2,1,0:T(8,128)(2,1)S(1)} %get-tuple-element.23) | data formatting | bytes 2621440
  61.5 0.7 %copy.16 = bf16[1,2,4,160,128]{4,3,2,1,0:T(8,128)(2,1)} copy(bf16[1,2,4,160,128]{4,3,2,1,0:T(8,128)(2,1)S(1)} %get-tuple-element.24) | data formatting | bytes 655360
  62.3 0.2 copy-done.5
  62.4 1.2 %copy.17 = f32[3,3,384,128]{3,2,1,0:T(8,128)} copy(f32[3,3,384,128]{3,2,1,0:T(8,128)S(1)} %copy-done.5) | data formatting | bytes 3538944
Async XLA Ops:
  0.6 1.2 %copy-start = (bf16[3,3,384,128]{3,2,1,0:T(8,128)(2,1)S(1)}, bf16[3,3,384,128]{3,2,1,0:T(8,128)(2,1)}, u32[]{:S(2)}) copy-start(bf16[3,3,384,128]{3,2,1,0:T(8,128)(2,1)} %ker_hbm.1) | copy-start | bytes 2654212
  1.8 1.0 %copy-start.1 = (bf16[1,2,4,160,128]{4,3,2,1,0:T(8,128)(2,1)S(1)}, bf16[1,2,4,160,128]{4,3,2,1,0:T(8,128)(2,1)}, u32[]{:S(2)}) copy-start(bf16[1,2,4,160,128]{4,3,2,1,0:T(8,128)(2,1)} %lat_hbm.1) | copy-start | bytes 983044
  2.8 0.7 %copy-start.2 = (f32[128]{0:T(128)S(1)}, f32[128]{0:T(128)}, u32[]{:S(2)}) copy-start(f32[128]{0:T(128)} %param.8) | copy-start | bytes 1540
  3.4 0.7 %copy-start.3 = (f32[128]{0:T(128)S(1)}, f32[128]{0:T(128)}, u32[]{:S(2)}) copy-start(f32[128]{0:T(128)} %param.9) | copy-start | bytes 1540
  4.1 0.7 %copy-start.4 = (f32[128]{0:T(128)S(1)}, f32[128]{0:T(128)}, u32[]{:S(2)}) copy-start(f32[128]{0:T(128)} %param.11) | copy-start | bytes 1540
  60.5 1.9 %copy-start.5 = (f32[3,3,384,128]{3,2,1,0:T(8,128)S(1)}, f32[3,3,384,128]{3,2,1,0:T(8,128)}, u32[]{:S(2)}) copy-start(f32[3,3,384,128]{3,2,1,0:T(8,128)} %get-tuple-element.25) | copy-start | bytes 5308420
where the time goes:
time: 64.5 us; the launch traced here: 63.6 us
  Pallas kernels  55.2 us (86%)
  local copies, waits for them, and re-layouts  7.77 us (12%)
  between operations  0.66 us (1%)
    pallas_call x1, Pallas kernels, local(): pl.pallas_call(functools.partial(body, float(count)), out_shape=(jax.Shap...  55.2 us
    unnamed x15, local copies, waits for them, and re-layouts  7.25 us

commit v1 on v0

--- a/solution.py
+++ b/solution.py
@@ -19,14 +19,15 @@
     count,
     lat_hbm,
     cot_hbm,
-    gain_ref,
-    bias_ref,
+    gain_hbm,
+    bias_hbm,
     ker_hbm,
-    kbias_ref,
-    up_hbm,
-    lg_hbm,
-    kg_hbm,
+    kbias_hbm,
+    up,
+    lg,
+    kg,
     small_ref,
+    vec,
     lat,
     cot,
     ker,
@@ -37,13 +38,10 @@
     line,
     pool,
     xhat_s,
-    dsilu_s,
     act_s,
     actt,
     acc,
-    up,
-    lg,
-    kg,
+    cacc,
     g,
     rc,
     s1,
@@ -57,7 +55,6 @@
     gr2,
     gr3,
     lsem,
-    osem,
     lat_ss,
     lat_rs,
     dc_ss,
@@ -107,6 +104,9 @@
         pltpu.make_async_copy(lat_hbm.at[0], lat.at[2:4, 1:5], lsem.at[1]),
         pltpu.make_async_copy(cot_hbm.at[0, 1], cot.at[1], lsem.at[2]),
         pltpu.make_async_copy(ker_hbm, ker, lsem.at[3]),
+        pltpu.make_async_copy(gain_hbm, vec.at[0:1], lsem.at[4]),
+        pltpu.make_async_copy(bias_hbm, vec.at[1:2], lsem.at[5]),
+        pltpu.make_async_copy(kbias_hbm, vec.at[2:3], lsem.at[6]),
     ]
     for c in loads:
         c.start()
@@ -204,18 +204,19 @@
         to = {"height": jnp.minimum(h + 1, 7) if down else jnp.maximum(h - 1, 0)}
         return remote(dc.at[f, src], dc.at[f, dst], dc_ss.at[n], dc_rs.at[n], to)
 
-    def lat_z(part):
+    def lat_z(t, part):
         rows = (slice(1, 2), slice(4, 5), slice(2, 4))[part]
+        n = 3 * t + part
         return remote(
-            lat.at[2:4, rows],
-            lat.at[0:2, rows],
-            lat_ss.at[part],
-            lat_rs.at[part],
+            lat.at[2 + t, rows],
+            lat.at[t, rows],
+            lat_ss.at[n],
+            lat_rs.at[n],
             {"tm": jnp.minimum(z + 1, 3)},
         )
 
     def lat_row(base, down):
-        n = 3 + base + down
+        n = 6 + base + down
         src, dst = (4, 0) if down else (1, 5)
         to = {"height": jnp.minimum(h + 1, 7) if down else jnp.maximum(h - 1, 0)}
         return remote(
@@ -230,42 +231,53 @@
 
     @pl.when(has_prev)
     def _():
-        for t in range(2):
-            for part in range(3):
-                dc_z(t, part).start()
-
-    @pl.when(has_up)
-    def _():
-        dc_row(0, 0).start()
-        dc_row(1, 0).start()
-        lat_row(2, 0).start()
-
-    @pl.when(has_down)
-    def _():
-        dc_row(0, 1).start()
-        dc_row(1, 1).start()
-        lat_row(2, 1).start()
+        for part in range(3):
+            dc_z(0, part).start()
 
     @pl.when(has_next)
     def _():
         for part in range(3):
-            lat_z(part).start()
+            lat_z(1, part).start()
+
+    for down, there in ((0, has_up), (1, has_down)):
+
+        @pl.when(there)
+        def _(down=down):
+            dc_row(0, down).start()
+            dc_row(1, down).start()
 
     exchange_wait(stat_h)
     st2[z] = tile_sum(st1, "h")
     stat_z = exchange_start(st2, "z", 8)
 
-    loads[3].wait()
-
-    def flip(n, carry):
-        i, j = n // 3, n % 3
-        for k in range(3):
-            kt[i, pl.ds(pl.multiple_of(j * 384 + k * 128, 128), 128), :] = ker[
-                i, j, k * 128 : (k + 1) * 128, :
-            ].T
-        return carry
-
-    lax.fori_loop(0, 9, flip, 0)
+    def forward(t):
+        @pl.when(has_next)
+        def _():
+            dc_z(t, 0).wait_recv()
+            dc_z(t, 1).wait_recv()
+            for down, there in ((0, has_up), (1, has_down)):
+
+                @pl.when(there)
+                def _(down=down):
+                    dc_row(2 + t, down).start()
+
+    forward(0)
+
+    @pl.when(has_prev)
+    def _():
+        for part in range(3):
+            dc_z(1, part).start()
+
+    @pl.when(has_next)
+    def _():
+        for part in range(3):
+            lat_z(0, part).start()
+
+    for down, there in ((0, has_up), (1, has_down)):
+
+        @pl.when(there)
+        def _(down=down):
+            lat_row(2, down).start()
 
     @pl.when(top)
     def _():
@@ -308,14 +320,54 @@
     special_rows(0)
     special_rows(3)
 
-    @pl.when(first)
-    def _():
-        def add(r, carry):
-            dslab[1, r] = dslab[0, r] + dslab[3, r]
+    def first_slot(slot, a, b):
+        @pl.when(first)
+        def _():
+            def add(r, carry):
+                dslab[slot, r] = dslab[a, r] + dslab[b, r]
+                return carry
+
+            lax.fori_loop(0, 6, add, 0)
+            special_rows(slot)
+
+    first_slot(1, 0, 3)
+
+    @pl.when(last)
+    def _():
+        for f in range(2, 4):
+            for r in range(6):
+                dc[f, r] = jnp.zeros((160, 128), BF16)
+
+    def ahead_inner(t):
+        @pl.when(has_next)
+        def _():
+            dc_z(t, 2).wait_recv()
+
+        def inner(r, carry):
+            grad_row(4 + t, 2 + t, r)
             return carry
 
-        lax.fori_loop(0, 6, add, 0)
-        special_rows(1)
+        lax.fori_loop(1, 5, inner, 0)
+
+    def ahead_outer(t):
+        @pl.when(has_next)
+        def _():
+            @pl.when(has_up)
+            def _():
+                dc_row(2 + t, 1).wait_recv()
+
+            @pl.when(has_down)
+            def _():
+                dc_row(2 + t, 0).wait_recv()
+
+        def outer(n, carry):
+            grad_row(4 + t, 2 + t, 5 * n)
+            return carry
+
+        lax.fori_loop(0, 2, outer, 0)
+        special_rows(4 + t)
+
+    ahead_inner(0)
 
     row_t = jnp.where(top, 6, 2)
     row_b = jnp.where(bottom, 7, 3)
@@ -350,20 +402,42 @@
     sums = by_group(tile_sum(st2, "z")) / count
     mean = sums[0:1]
     rstd = lax.rsqrt(sums[1:2] - mean * mean + 1e-6)
-    gain = gain_ref[...]
-    shift = bias_ref[...]
-
-    def act_row(f, r, own):
-        v = (lat[f, r].astype(F32) - mean) * rstd
-        pre = v * gain + shift
-        sig = 1.0 / (1.0 + jnp.exp(-pre))
-        a = pre * sig
-        if own:
-            n = (f - 2) * 4 + r - 1
-            rows = pl.ds(pl.multiple_of(n * 160, 160), 160)
-            xhat_s[rows, :] = v
-            dsilu_s[rows, :] = sig * (1.0 + pre * (1.0 - sig))
-            act_s[rows, :] = a
+    for c in loads[4:]:
+        c.wait()
+    gain = vec[0:1]
+    shift = vec[1:2]
+    kbias = vec[2:3]
+
+    def normed(f, r):
+        return (lat[f, r].astype(F32) - mean) * rstd
+
+    def own_row(f, r, n):
+        pre = normed(f, r) * gain + shift
+        act_s[pl.ds(pl.multiple_of(n * 160, 160), 160), :] = pre / (1.0 + jnp.exp(-pre))
+
+    def own_rows(n, carry):
+        own_row(3 - n // 4, 1 + n % 4, n)
+        return carry
+
+    @pl.when(has_prev)
+    def _():
+        for part in range(3):
+            lat_z(1, part).wait_recv()
+
+    lax.fori_loop(0, 12, own_rows, 0)
+
+    def transposed(n, carry):
+        rows = pl.ds(pl.multiple_of(n * 128, 128), 128)
+        actt[:, rows] = act_s[rows, :].T.astype(BF16)
+        return carry
+
+    lax.fori_loop(0, 15, transposed, 0)
+
+    @pl.when(first)
+    def _():
+        actt[:, 1280:1920] = jnp.zeros((128, 640), BF16)
+
+    def act_line(f, r, a):
         line[8:168, :] = a
         line[7:8, :] = a[0:1]
         line[168:169, :] = a[159:160]
@@ -371,23 +445,21 @@
         aslab[f, r, :, 128:256] = a.astype(BF16)
         aslab[f, r, :, 256:384] = line[9:169, :].astype(BF16)
 
-    def own_rows(n, carry):
-        act_row(2 + n // 4, 1 + n % 4, True)
-        return carry
-
-    lax.fori_loop(0, 8, own_rows, 0)
-
-    def transposed(n, carry):
-        rows = pl.ds(pl.multiple_of(n * 128, 128), 128)
-        actt[:, rows] = act_s[rows, :].T.astype(BF16)
-        return carry
-
-    lax.fori_loop(0, 10, transposed, 0)
+    def act_row(f, r):
+        pre = normed(f, r) * gain + shift
+        act_line(f, r, pre / (1.0 + jnp.exp(-pre)))
 
     def weight_grad(i):
         for j in range(3):
-            right = jnp.concatenate([taken(slot_of[0, i], j), taken(slot_of[1, i], j)], axis=0)
-            part = jnp.dot(actt[...], right, preferred_element_type=F32)
+            other = taken(3 if i == 0 else slot_of[1, i], j)
+            mine = taken(slot_of[0, i], j)
+            if i == 0:
+                right = jnp.concatenate([mine, other], axis=0)
+                left = actt[:, 640:1920]
+            else:
+                right = jnp.concatenate([other, mine], axis=0)
+                left = actt[:, 0:1280]
+            part = jnp.dot(left, right, preferred_element_type=F32)
             g[i, :, :, j * 384 : (j + 1) * 384] = part.astype(BF16).reshape(8, 16, 384)
 
     copies = {}
@@ -473,8 +545,6 @@
         c.start()
         copies[i, 5] = [c]
 
-    outs = []
-
     def finish(i):
         for c in copies[i, 5]:
             c.wait_recv()
@@ -483,79 +553,47 @@
             kg[i, j, k * 128 : (k + 1) * 128, :] = (
                 fin[i, :, :, n * 128 : (n + 1) * 128].reshape(128, 128).astype(F32)
             )
-        c = pltpu.make_async_copy(kg.at[i], kg_hbm.at[i], osem.at[i])
-        c.start()
-        outs.append(c)
 
     weight_grad(2)
     copy_c(2)
-
-    @pl.when(last)
-    def _():
-        for f in range(2, 4):
-            for r in range(6):
-                dc[f, r] = jnp.zeros((160, 128), BF16)
-
-    def ahead(t):
-        f = 2 + t
-
-        @pl.when(has_next)
-        def _():
-            dc_z(t, 0).wait_recv()
-            dc_z(t, 1).wait_recv()
-
-            @pl.when(has_up)
-            def _():
-                dc_row(f, 0).start()
-
-            @pl.when(has_down)
-            def _():
-                dc_row(f, 1).start()
-
-            dc_z(t, 2).wait_recv()
-
-        def inner(r, carry):
-            grad_row(4 + t, f, r)
-            return carry
-
-        lax.fori_loop(1, 5, inner, 0)
-
-        @pl.when(has_next)
-        def _():
-            @pl.when(has_up)
-            def _():
-                dc_row(f, 1).wait_recv()
-
-            @pl.when(has_down)
-            def _():
-                dc_row(f, 0).wait_recv()
-
-        def outer(n, carry):
-            grad_row(4 + t, f, 5 * n)
-            return carry
-
-        lax.fori_loop(0, 2, outer, 0)
-        special_rows(4 + t)
-
-    ahead(0)
-
-    @pl.when(first)
-    def _():
-        def add(r, carry):
-            dslab[2, r] = dslab[1, r] + dslab[4, r]
-            return carry
-
-        lax.fori_loop(0, 6, add, 0)
-        special_rows(2)
-
-    reduce_1(2)
+    ahead_outer(0)
+    first_slot(2, 1, 4)
     weight_grad(1)
     copy_c(1)
-    ahead(1)
-    reduce_2(2)
-    reduce_1(1)
     weight_grad(0)
     copy_c(0)
+
+    forward(1)
+
+    @pl.when(has_prev)
+    def _():
+        lat_z(0, 0).wait_recv()
+        lat_z(0, 1).wait_recv()
+        for down, there in ((0, has_up), (1, has_down)):
+
+            @pl.when(there)
+            def _(down=down):
+                lat_row(0, down).start()
+
+        lat_z(0, 2).wait_recv()
+
+    reduce_1(2)
+    reduce_1(1)
+    loads[3].wait()
+
+    def flip(n, carry):
+        i, j = n // 3, n % 3
+        for k in range(3):
+            kt[i, pl.ds(pl.multiple_of(j * 384 + k * 128, 128), 128), :] = ker[
+                i, j, k * 128 : (k + 1) * 128, :
+            ].T
+        return carry
+
+    lax.fori_loop(0, 9, flip, 0)
+
+    reduce_1(0)
+    ahead_inner(1)
+    ahead_outer(1)
 
     def data_grad(p):
         rows = slice(p * 640, (p + 1) * 640)
@@ -567,25 +605,25 @@
             acc[rows, :] = part if i == 2 else acc[rows, :] + part
 
     data_grad(0)
-    reduce_3(2)
-    reduce_2(1)
-    reduce_1(0)
     data_grad(1)
 
     def through(n, carry):
         a, b = carry
         rows = pl.ds(pl.multiple_of(n * 160, 160), 160)
-        d = acc[rows, :] * dsilu_s[rows, :]
+        v = normed(2 + n // 4, 1 + n % 4)
+        pre = v * gain + shift
+        sig = 1.0 / (1.0 + jnp.exp(-pre))
+        d = acc[rows, :] * (sig * (1.0 + pre * (1.0 - sig)))
         acc[rows, :] = d
-        b = b + (d * xhat_s[rows, :]).reshape(20, 8, 128).sum(axis=0)
+        xhat_s[rows, :] = v
+        b = b + (d * v).reshape(20, 8, 128).sum(axis=0)
         return a + d.reshape(20, 8, 128).sum(axis=0), b
 
     d_sum, dx_sum = lax.fori_loop(0, 8, through, (zero8, zero8))
     gr1[h] = rows_of(d_sum, dx_sum, bias_total)
     grad_h = exchange_start(gr1, "h", 12)
-    gather_1(2)
-    reduce_3(1)
-    reduce_2(0)
+    for i in (2, 1, 0):
+        reduce_2(i)
 
     @pl.when(top)
     def _():
@@ -607,19 +645,6 @@
 
     @pl.when(has_prev)
     def _():
-        lat_z(0).wait_recv()
-        lat_z(1).wait_recv()
-
-        @pl.when(has_up)
-        def _():
-            lat_row(0, 0).start()
-
-        @pl.when(has_down)
-        def _():
-            lat_row(0, 1).start()
-
-        lat_z(2).wait_recv()
-
         @pl.when(top)
         def _():
             for f in range(2):
@@ -644,44 +669,27 @@
             for r in range(6):
                 lat[f, r] = lat[2, r]
 
+    def own_lines(n, carry):
+        rows = pl.ds(pl.multiple_of(n * 160, 160), 160)
+        act_line(3 - n // 4, 1 + n % 4, act_s[rows, :])
+        return carry
+
+    lax.fori_loop(0, 8, own_lines, 0)
+
+    def edge_act(n, carry):
+        act_row(2 + n // 2, 5 * (n % 2))
+        return carry
+
+    lax.fori_loop(0, 4, edge_act, 0)
+
+    def past_act(n, carry):
+        act_row(n // 6, n % 6)
+        return carry
+
+    lax.fori_loop(0, 12, past_act, 0)
     exchange_wait(grad_h)
     gr2[z] = tile_sum(gr1, "h")
     grad_z = exchange_start(gr2, "z", 20)
-
-    def edge_act(n, carry):
-        act_row(2 + n // 2, 5 * (n % 2), False)
-        return carry
-
-    lax.fori_loop(0, 4, edge_act, 0)
-
-    def past_act(n, carry):
-        act_row(n // 6, n % 6, False)
-        return carry
-
-    lax.fori_loop(0, 12, past_act, 0)
-    gather_c(2)
-    gather_1(1)
-    reduce_3(0)
-    exchange_wait(grad_z)
-    clip_sums = tile_sum(gr2, "z")
-    gr3[y] = clip_sums
-    grad_y = exchange_start(gr3, "y", 24)
-
-    means = by_group(clip_sums * gain) / count
-    mean_a, mean_b = means[0:1], means[1:2]
-
-    def latent_grad(n, carry):
-        rows = pl.ds(pl.multiple_of(n * 160, 160), 160)
-        v = rstd * (acc[rows, :] * gain - mean_a - xhat_s[rows, :] * mean_b)
-        lg[n // 4, n % 4] = v.astype(BF16)
-        return carry
-
-    lax.fori_loop(0, 8, latent_grad, 0)
-    c = pltpu.make_async_copy(lg, lg_hbm.at[0], osem.at[3])
-    c.start()
-    outs.append(c)
-
-    kbias = kbias_ref[...]
 
     def conv(t):
         rows = slice(t * 640, (t + 1) * 640)
@@ -690,32 +698,46 @@
                 [aslab[t + i, j : j + 4].reshape(640, 384) for j in range(3)], axis=1
             )
             part = jnp.dot(left, ker[i].reshape(1152, 128), preferred_element_type=F32)
-            act_s[rows, :] = part if i == 0 else act_s[rows, :] + part
+            cacc[rows, :] = part if i == 0 else cacc[rows, :] + part
 
         def expand(r, carry):
-            v = act_s[pl.ds(pl.multiple_of((t * 4 + r) * 160, 160), 160), :] + kbias
+            v = cacc[pl.ds(pl.multiple_of((t * 4 + r) * 160, 160), 160), :] + kbias
             pool[pl.ds(0, 160, stride=2), :] = v
             pool[pl.ds(1, 160, stride=2), :] = v
             w = pool[...].astype(BF16)
-            up[t, 2 * r] = w
-            up[t, 2 * r + 1] = w
+            up[0, t, 2 * r] = w
+            up[0, t, 2 * r + 1] = w
             return carry
 
         lax.fori_loop(0, 4, expand, 0)
-        c = pltpu.make_async_copy(up.at[t], up_hbm.at[0, t], osem.at[4 + t])
-        c.start()
-        outs.append(c)
-
+
+    for i in (2, 1, 0):
+        reduce_3(i)
     conv(0)
-    finish(2)
-    gather_c(1)
-    gather_1(0)
+    exchange_wait(grad_z)
+    clip_sums = tile_sum(gr2, "z")
+    gr3[y] = clip_sums
+    grad_y = exchange_start(gr3, "y", 24)
+
+    means = by_group(clip_sums * gain) / count
+    mean_a, mean_b = means[0:1], means[1:2]
+
+    def latent_grad(n, carry):
+        rows = pl.ds(pl.multiple_of(n * 160, 160), 160)
+        v = rstd * (acc[rows, :] * gain - mean_a - xhat_s[rows, :] * mean_b)
+        lg[0, n // 4, n % 4] = v.astype(BF16)
+        return carry
+
+    lax.fori_loop(0, 8, latent_grad, 0)
+    for i in (2, 1, 0):
+        gather_1(i)
     conv(1)
-    finish(1)
-    gather_c(0)
     exchange_wait(grad_y)
     small_ref[...] = tile_sum(gr3, "y")
-    finish(0)
+    for i in (2, 1, 0):
+        gather_c(i)
+    for i in (2, 1, 0):
+        finish(i)
 
     for group in (stat_h, stat_z, grad_h, grad_z, grad_y, *copies.values()):
         for c in group:
@@ -729,8 +751,9 @@
 
     @pl.when(has_next)
     def _():
-        for part in range(3):
-            lat_z(part).wait_send()
+        for t in range(2):
+            for part in range(3):
+                lat_z(t, part).wait_send()
 
     for down, there in ((0, has_up), (1, has_down)):
 
@@ -749,26 +772,45 @@
             def _():
                 lat_row(0, down).wait_send()
 
-    for c in outs:
+
+def emit(up, lg, kg, small, up_out, lg_out, kg_out, bias_out, gain_out, shift_out, sem):
+    copies = [
+        pltpu.make_async_copy(src, dst, sem.at[n])
+        for n, (src, dst) in enumerate(
+            (
+                (up, up_out),
+                (lg, lg_out),
+                (kg, kg_out),
+                (small.at[2:3], bias_out),
+                (small.at[1:2], gain_out),
+                (small.at[0:1], shift_out),
+            )
+        )
+    ]
+    for c in copies:
+        c.start()
+    for c in copies:
         c.wait()
 
 
 def local(latents, cotangent, gain, bias, kernel, kernel_bias):
     count = 8 * 32 * 160 * (128 // GROUPS)
-    hbm = pl.BlockSpec(memory_space=pl.ANY)
+    hbm = pl.BlockSpec(memory_space=pltpu.HBM)
     vmem = pl.BlockSpec(memory_space=pltpu.VMEM)
     dma = pltpu.SemaphoreType.DMA
+    shapes = (
+        jax.ShapeDtypeStruct((1, 2, 8, 320, 128), BF16),
+        jax.ShapeDtypeStruct((1, 2, 4, 160, 128), BF16),
+        jax.ShapeDtypeStruct((3, 3, 384, 128), F32),
+    )
+    operands = (latents, cotangent, gain[None], bias[None], kernel, kernel_bias[None])
     up, lg, kg, small = pl.pallas_call(
         functools.partial(body, float(count)),
-        out_shape=(
-            jax.ShapeDtypeStruct((1, 2, 8, 320, 128), BF16),
-            jax.ShapeDtypeStruct((1, 2, 4, 160, 128), BF16),
-            jax.ShapeDtypeStruct((3, 3, 384, 128), F32),
-            jax.ShapeDtypeStruct((8, 128), F32),
-        ),
-        in_specs=[hbm, hbm, vmem, vmem, hbm, vmem],
-        out_specs=(hbm, hbm, hbm, vmem),
+        out_shape=(*shapes, jax.ShapeDtypeStruct((8, 128), F32)),
+        in_specs=[hbm] * 6,
+        out_specs=(vmem,) * 4,
         scratch_shapes=[
+            pltpu.VMEM((8, 128), F32),
             pltpu.VMEM((4, 6, 160, 128), BF16),
             pltpu.VMEM((2, 8, 320, 128), BF16),
             pltpu.VMEM((3, 3, 384, 128), BF16),
@@ -779,13 +821,10 @@
             pltpu.VMEM((176, 128), F32),
             pltpu.VMEM((320, 128), F32),
             pltpu.VMEM((1280, 128), F32),
+            pltpu.VMEM((1920, 128), F32),
+            pltpu.VMEM((128, 1920), BF16),
             pltpu.VMEM((1280, 128), F32),
             pltpu.VMEM((1280, 128), F32),
-            pltpu.VMEM((128, 1280), BF16),
-            pltpu.VMEM((1280, 128), F32),
-            pltpu.VMEM((2, 8, 320, 128), BF16),
-            pltpu.VMEM((2, 4, 160, 128), BF16),
-            pltpu.VMEM((3, 3, 384, 128), F32),
             pltpu.VMEM((3, 8, 16, 1152), BF16),
             pltpu.VMEM((3, 4, 16, 1152), BF16),
             pltpu.VMEM((3, 4, 16, 1152), BF16),
@@ -798,10 +837,9 @@
             pltpu.VMEM((8, 8, 128), F32),
             pltpu.VMEM((4, 8, 128), F32),
             pltpu.VMEM((4, 8, 128), F32),
-            dma((4,)),
-            dma((6,)),
             dma((7,)),
-            dma((7,)),
+            dma((10,)),
+            dma((10,)),
             dma((14,)),
             dma((14,)),
             dma((28,)),
@@ -810,11 +848,20 @@
             dma((3, 14)),
         ],
         compiler_params=pltpu.CompilerParams(
-            collective_id=0, has_side_effects=True, vmem_limit_bytes=50 * 1024 * 1024
+            collective_id=0, has_side_effects=True, vmem_limit_bytes=40 * 1024 * 1024
         ),
         cost_estimate=pl.CostEstimate(flops=3 * 2 * 1280 * 3456 * 128, bytes_accessed=6000000, transcendentals=500000),
-    )(latents, cotangent, gain[None], bias[None], kernel, kernel_bias[None])
-    return up, lg, kg, small[2], small[1], small[0]
+    )(*(pltpu.with_memory_space_constraint(a, pltpu.HBM) for a in operands))
+    row = jax.ShapeDtypeStruct((1, 128), F32)
+    up, lg, kg, bias_grad, gain_grad, shift_grad = pl.pallas_call(
+        emit,
+        out_shape=(*shapes, row, row, row),
+        in_specs=[vmem] * 4,
+        out_specs=(hbm,) * 6,
+        scratch_shapes=[dma((6,))],
+        cost_estimate=pl.CostEstimate(flops=0, bytes_accessed=3500000, transcendentals=0),
+    )(*(pltpu.with_memory_space_constraint(a, pltpu.VMEM) for a in (up, lg, kg, small)))
+    return up, lg, kg, bias_grad[0], gain_grad[0], shift_grad[0]
 
 
 def solution(mesh):

time: 64.5 us -> 43.9 us (0.68); the launches traced: 63.6 us -> 43.8 us
  Pallas kernels: 55.2 us -> 43.2 us
  local copies, waits for them, and re-layouts: 7.77 us -> 0 us
    pallas_call x1 -> x2, Pallas kernels: 55.2 us -> 43.2 us  [the longest x1 41.3 us: local(): pl.pallas_call(functools.partial(body, float(count)), out_shape=(*shapes,...]
    unnamed x15 -> x0, local copies, waits for them, and re-layouts: 7.25 us -> none
where the time goes in v1:
time: 43.9 us; the launch traced here: 43.8 us
  Pallas kernels  43.2 us (98%)
  between operations  0.64 us (1%)
    pallas_call x1, Pallas kernels, local(): pl.pallas_call(functools.partial(body, float(count)), out_shape=(*shapes,...  41.3 us
    pallas_call x1, Pallas kernels, local(): pl.pallas_call(emit, out_shape=(*shapes, row, row, row), in_specs=[vmem]...  1.81 us

profile of v1, /device:TPU:1, one launch (start us, length us, event | category | flops | bytes accessed | tf_op | source)
XLA Modules:
  0.0 43.8 jit_solution(9425006605582384618)
XLA Ops:
  0.6 41.3 %shard_map.109 = (bf16[1,2,8,320,128]{4,3,2,1,0:T(8,128)(2,1)S(1)}, bf16[1,2,4,160,128]{4,3,2,1,0:T(8,128)(2,1)S(1)}, f32[3,3,384,128]{3,2,1,0:T(8,128)S(1)}, f32[8,128]{1,0:T(8,128)S(1)}) custom-call(bf16[1,2,4,160,128]{4,3,2,1,0:T(8,128)(2,1)} %lat_hbm.1, bf16[1,2,8,320,128]{4,3,2,1,0:T(8,128)(2,1)} %cot_hbm.1, f32[1,128]{1,0:T(1,128)} %bitcast.6, ...), custom_call_target="tpu_custom_call" | custom-call | flops 3397386240 | bytes 6000000 | tf_op jit(solution)/shard_map/pallas_call | solution.py:807
  42.0 1.8 %shard_map.110 = (bf16[1,2,8,320,128]{4,3,2,1,0:T(8,128)(2,1)}, bf16[1,2,4,160,128]{4,3,2,1,0:T(8,128)(2,1)}, f32[3,3,384,128]{3,2,1,0:T(8,128)}, f32[1,128]{1,0...) custom-call(bf16[1,2,8,320,128]{4,3,2,1,0:T(8,128)(2,1)S(1)} %get-tuple-element.16.up, ...), custom_call_target="tpu_custom_call" | custom-call | bytes 3500000 | tf_op jit(solution)/shard_map/pallas_call | solution.py:856

commit v2 on v1

--- a/solution.py
+++ b/solution.py
@@ -40,6 +40,7 @@
     xhat_s,
     act_s,
     actt,
+    pastt,
     acc,
     cacc,
     g,
@@ -93,15 +94,9 @@
             src_ref=src, dst_ref=dst, send_sem=ss, recv_sem=rs, device_id=to, device_id_type=MESH
         )
 
-    barrier = pltpu.get_barrier_semaphore()
-    greeted = [peer("h", d) for d in range(1, 8)]
-    greeted += [peer("z", d) for d in range(1, 4)] + [peer("y", d) for d in range(1, 4)]
-    for to in greeted:
-        pl.semaphore_signal(barrier, inc=1, device_id=to, device_id_type=MESH)
-
     loads = [
-        pltpu.make_async_copy(cot_hbm.at[0, 0], cot.at[0], lsem.at[0]),
-        pltpu.make_async_copy(lat_hbm.at[0], lat.at[2:4, 1:5], lsem.at[1]),
+        pltpu.make_async_copy(lat_hbm.at[0], lat.at[2:4, 1:5], lsem.at[0]),
+        pltpu.make_async_copy(cot_hbm.at[0, 0], cot.at[0], lsem.at[1]),
         pltpu.make_async_copy(cot_hbm.at[0, 1], cot.at[1], lsem.at[2]),
         pltpu.make_async_copy(ker_hbm, ker, lsem.at[3]),
         pltpu.make_async_copy(gain_hbm, vec.at[0:1], lsem.at[4]),
@@ -110,6 +105,12 @@
     ]
     for c in loads:
         c.start()
+
+    barrier = pltpu.get_barrier_semaphore()
+    greeted = [peer("h", d) for d in range(1, 8)]
+    greeted += [peer("z", d) for d in range(1, 4)] + [peer("y", d) for d in range(1, 4)]
+    for to in greeted:
+        pl.semaphore_signal(barrier, inc=1, device_id=to, device_id_type=MESH)
 
     row16 = lax.broadcasted_iota(jnp.int32, (16, 128), 0)
 
@@ -141,11 +142,6 @@
         return lax.fori_loop(0, 4, step, total)
 
     loads[0].wait()
-    bias_total = pool_frame(0, jnp.zeros((8, 128), F32))
-    loads[2].wait()
-    bias_total = pool_frame(1, bias_total)
-
-    loads[1].wait()
 
     def stat_step(n, carry):
         s, q = carry
@@ -229,21 +225,38 @@
 
     stat_h = exchange_start(st1, "h", 0)
 
+    @pl.when(has_next)
+    def _():
+        for part in range(3):
+            lat_z(1, part).start()
+
+    for down, there in ((0, has_up), (1, has_down)):
+
+        @pl.when(there)
+        def _(down=down):
+            lat_row(2, down).start()
+
+    loads[1].wait()
+    bias_total = pool_frame(0, zero8)
+
     @pl.when(has_prev)
     def _():
         for part in range(3):
             dc_z(0, part).start()
-
-    @pl.when(has_next)
-    def _():
-        for part in range(3):
-            lat_z(1, part).start()
 
     for down, there in ((0, has_up), (1, has_down)):
 
         @pl.when(there)
         def _(down=down):
             dc_row(0, down).start()
+
+    loads[2].wait()
+    bias_total = pool_frame(1, bias_total)
+
+    for down, there in ((0, has_up), (1, has_down)):
+
+        @pl.when(there)
+        def _(down=down):
             dc_row(1, down).start()
 
     exchange_wait(stat_h)
@@ -261,8 +274,6 @@
                 def _(down=down):
                     dc_row(2 + t, down).start()
 
-    forward(0)
-
     @pl.when(has_prev)
     def _():
         for part in range(3):
@@ -272,12 +283,6 @@
     def _():
         for part in range(3):
             lat_z(0, part).start()
-
-    for down, there in ((0, has_up), (1, has_down)):
-
-        @pl.when(there)
-        def _(down=down):
-            lat_row(2, down).start()
 
     @pl.when(top)
     def _():
@@ -320,17 +325,21 @@
     special_rows(0)
     special_rows(3)
 
-    def first_slot(slot, a, b):
+    def first_slot(slot, a, b, inner):
         @pl.when(first)
         def _():
-            def add(r, carry):
+            def add(n, carry):
+                r = n if inner else 5 * n
                 dslab[slot, r] = dslab[a, r] + dslab[b, r]
                 return carry
 
-            lax.fori_loop(0, 6, add, 0)
-            special_rows(slot)
-
-    first_slot(1, 0, 3)
+            if inner:
+                lax.fori_loop(1, 5, add, 0)
+            else:
+                lax.fori_loop(0, 2, add, 0)
+                special_rows(slot)
+
+    first_slot(1, 0, 3, True)
 
     @pl.when(last)
     def _():
@@ -367,7 +376,27 @@
         lax.fori_loop(0, 2, outer, 0)
         special_rows(4 + t)
 
+    forward(0)
     ahead_inner(0)
+    first_slot(2, 1, 4, True)
+
+    @pl.when(top)
+    def _():
+        for f in range(2, 4):
+            lat[f, 0] = lat[f, 1]
+
+    @pl.when(bottom)
+    def _():
+        for f in range(2, 4):
+            lat[f, 5] = lat[f, 4]
+
+    @pl.when(has_up)
+    def _():
+        lat_row(2, 1).wait_recv()
+
+    @pl.when(has_down)
+    def _():
+        lat_row(2, 0).wait_recv()
 
     row_t = jnp.where(top, 6, 2)
     row_b = jnp.where(bottom, 7, 3)
@@ -416,7 +445,7 @@
         act_s[pl.ds(pl.multiple_of(n * 160, 160), 160), :] = pre / (1.0 + jnp.exp(-pre))
 
     def own_rows(n, carry):
-        own_row(3 - n // 4, 1 + n % 4, n)
+        own_row(3 - n // 6, jnp.where(n < 12, n % 6, n - 11), n)
         return carry
 
     @pl.when(has_prev)
@@ -424,18 +453,26 @@
         for part in range(3):
             lat_z(1, part).wait_recv()
 
-    lax.fori_loop(0, 12, own_rows, 0)
-
-    def transposed(n, carry):
-        rows = pl.ds(pl.multiple_of(n * 128, 128), 128)
-        actt[:, rows] = act_s[rows, :].T.astype(BF16)
-        return carry
-
-    lax.fori_loop(0, 15, transposed, 0)
+    lax.fori_loop(0, 16, own_rows, 0)
+
+    eye_a = lax.broadcasted_iota(jnp.int32, (128, 128), 0)
+    eye_b = lax.broadcasted_iota(jnp.int32, (128, 128), 1)
+    eye = jnp.where(eye_a == eye_b, 1.0, 0.0).astype(BF16)
+
+    def turned(start):
+        v = act_s[start : start + 640, :].astype(BF16)
+        return lax.dot_general(
+            eye, v, (((1,), (1,)), ((), ())), preferred_element_type=F32
+        ).astype(BF16)
+
+    for j in range(3):
+        for p in range(2):
+            actt[j, :, p * 640 : (p + 1) * 640] = turned(p * 960 + j * 160)
+    pastt[...] = turned(1920)
 
     @pl.when(first)
     def _():
-        actt[:, 1280:1920] = jnp.zeros((128, 640), BF16)
+        pastt[...] = jnp.zeros((128, 640), BF16)
 
     def act_line(f, r, a):
         line[8:168, :] = a
@@ -451,16 +488,16 @@
 
     def weight_grad(i):
         for j in range(3):
-            other = taken(3 if i == 0 else slot_of[1, i], j)
-            mine = taken(slot_of[0, i], j)
+            mine = dslab[pl.ds(slot_of[0, i], 1), 1:5].reshape(640, 384)
             if i == 0:
-                right = jnp.concatenate([mine, other], axis=0)
-                left = actt[:, 640:1920]
+                right = jnp.concatenate([mine, taken(3, j)], axis=0)
+                left = jnp.concatenate([actt[j, :, 640:1280], pastt[...]], axis=1)
             else:
+                other = dslab[slot_of[1, i], 1:5].reshape(640, 384)
                 right = jnp.concatenate([other, mine], axis=0)
-                left = actt[:, 0:1280]
+                left = actt[j]
             part = jnp.dot(left, right, preferred_element_type=F32)
-            g[i, :, :, j * 384 : (j + 1) * 384] = part.astype(BF16).reshape(8, 16, 384)
+            g[i, :, :, j * 384 : (j + 1) * 384] = part.reshape(8, 16, 384)
 
     copies = {}
 
@@ -478,7 +515,7 @@
     def reduce_1(i):
         for c in copies[i, 0]:
             c.wait_recv()
-        s1[i] = (g[i, pl.ds(core * 4, 4)].astype(F32) + rc[i].astype(F32)).astype(BF16)
+        s1[i] = (g[i, pl.ds(core * 4, 4)] + rc[i]).astype(BF16)
         axis = ORDER[i][0]
         me = place[axis]
         copies[i, 1] = []
@@ -556,14 +593,13 @@
 
     weight_grad(2)
     copy_c(2)
-    ahead_outer(0)
-    first_slot(2, 1, 4)
     weight_grad(1)
     copy_c(1)
+    reduce_1(2)
+    forward(1)
     weight_grad(0)
     copy_c(0)
-
-    forward(1)
+    reduce_1(1)
 
     @pl.when(has_prev)
     def _():
@@ -575,10 +611,7 @@
             def _(down=down):
                 lat_row(0, down).start()
 
-        lat_z(0, 2).wait_recv()
-
-    reduce_1(2)
-    reduce_1(1)
+
     loads[3].wait()
 
     def flip(n, carry):
@@ -592,8 +625,22 @@
     lax.fori_loop(0, 9, flip, 0)
 
     reduce_1(0)
+
+    def own_lines(n, carry):
+        rows = pl.ds(pl.multiple_of(n * 160, 160), 160)
+        act_line(3 - n // 6, n % 6, act_s[rows, :])
+        return carry
+
+    lax.fori_loop(0, 12, own_lines, 0)
+
     ahead_inner(1)
+    reduce_2(2)
+    ahead_outer(0)
+    first_slot(1, 0, 3, False)
+    first_slot(2, 1, 4, False)
     ahead_outer(1)
+    reduce_2(1)
+    reduce_2(0)
 
     def data_grad(p):
         rows = slice(p * 640, (p + 1) * 640)
@@ -623,28 +670,12 @@
     gr1[h] = rows_of(d_sum, dx_sum, bias_total)
     grad_h = exchange_start(gr1, "h", 12)
     for i in (2, 1, 0):
-        reduce_2(i)
-
-    @pl.when(top)
-    def _():
-        for f in range(2, 4):
-            lat[f, 0] = lat[f, 1]
-
-    @pl.when(bottom)
-    def _():
-        for f in range(2, 4):
-            lat[f, 5] = lat[f, 4]
-
-    @pl.when(has_up)
-    def _():
-        lat_row(2, 1).wait_recv()
-
-    @pl.when(has_down)
-    def _():
-        lat_row(2, 0).wait_recv()
+        reduce_3(i)
 
     @pl.when(has_prev)
     def _():
+        lat_z(0, 2).wait_recv()
+
         @pl.when(top)
         def _():
             for f in range(2):
@@ -669,28 +700,11 @@
             for r in range(6):
                 lat[f, r] = lat[2, r]
 
-    def own_lines(n, carry):
-        rows = pl.ds(pl.multiple_of(n * 160, 160), 160)
-        act_line(3 - n // 4, 1 + n % 4, act_s[rows, :])
-        return carry
-
-    lax.fori_loop(0, 8, own_lines, 0)
-
-    def edge_act(n, carry):
-        act_row(2 + n // 2, 5 * (n % 2))
-        return carry
-
-    lax.fori_loop(0, 4, edge_act, 0)
-
     def past_act(n, carry):
         act_row(n // 6, n % 6)
         return carry
 
     lax.fori_loop(0, 12, past_act, 0)
-    exchange_wait(grad_h)
-    gr2[z] = tile_sum(gr1, "h")
-    grad_z = exchange_start(gr2, "z", 20)
-
     def conv(t):
         rows = slice(t * 640, (t + 1) * 640)
         for i in range(3):
@@ -700,6 +714,7 @@
             part = jnp.dot(left, ker[i].reshape(1152, 128), preferred_element_type=F32)
             cacc[rows, :] = part if i == 0 else cacc[rows, :] + part
 
+    def upsample(t):
         def expand(r, carry):
             v = cacc[pl.ds(pl.multiple_of((t * 4 + r) * 160, 160), 160), :] + kbias
             pool[pl.ds(0, 160, stride=2), :] = v
@@ -711,9 +726,15 @@
 
         lax.fori_loop(0, 4, expand, 0)
 
+    conv(0)
+    exchange_wait(grad_h)
+    gr2[z] = tile_sum(gr1, "h")
+    grad_z = exchange_start(gr2, "z", 20)
+
     for i in (2, 1, 0):
-        reduce_3(i)
-    conv(0)
+        gather_1(i)
+    upsample(0)
+    conv(1)
     exchange_wait(grad_z)
     clip_sums = tile_sum(gr2, "z")
     gr3[y] = clip_sums
@@ -730,14 +751,12 @@
 
     lax.fori_loop(0, 8, latent_grad, 0)
     for i in (2, 1, 0):
-        gather_1(i)
-    conv(1)
+        gather_c(i)
+    upsample(1)
+    for i in (2, 1, 0):
+        finish(i)
     exchange_wait(grad_y)
     small_ref[...] = tile_sum(gr3, "y")
-    for i in (2, 1, 0):
-        gather_c(i)
-    for i in (2, 1, 0):
-        finish(i)
 
     for group in (stat_h, stat_z, grad_h, grad_z, grad_y, *copies.values()):
         for c in group:
@@ -774,18 +793,16 @@
 
 
 def emit(up, lg, kg, small, up_out, lg_out, kg_out, bias_out, gain_out, shift_out, sem):
+    pairs = [(kg.at[i], kg_out.at[i]) for i in range(3)]
+    pairs += [(up.at[0, t], up_out.at[0, t]) for t in range(2)]
+    pairs += [
+        (lg, lg_out),
+        (small.at[2:3], bias_out),
+        (small.at[1:2], gain_out),
+        (small.at[0:1], shift_out),
+    ]
     copies = [
-        pltpu.make_async_copy(src, dst, sem.at[n])
-        for n, (src, dst) in enumerate(
-            (
-                (up, up_out),
-                (lg, lg_out),
-                (kg, kg_out),
-                (small.at[2:3], bias_out),
-                (small.at[1:2], gain_out),
-                (small.at[0:1], shift_out),
-            )
-        )
+        pltpu.make_async_copy(src, dst, sem.at[n]) for n, (src, dst) in enumerate(pairs)
     ]
     for c in copies:
         c.start()
@@ -821,12 +838,13 @@
             pltpu.VMEM((176, 128), F32),
             pltpu.VMEM((320, 128), F32),
             pltpu.VMEM((1280, 128), F32),
-            pltpu.VMEM((1920, 128), F32),
-            pltpu.VMEM((128, 1920), BF16),
+            pltpu.VMEM((2560, 128), F32),
+            pltpu.VMEM((3, 128, 1280), BF16),
+            pltpu.VMEM((128, 640), BF16),
             pltpu.VMEM((1280, 128), F32),
             pltpu.VMEM((1280, 128), F32),
-            pltpu.VMEM((3, 8, 16, 1152), BF16),
-            pltpu.VMEM((3, 4, 16, 1152), BF16),
+            pltpu.VMEM((3, 8, 16, 1152), F32),
+            pltpu.VMEM((3, 4, 16, 1152), F32),
             pltpu.VMEM((3, 4, 16, 1152), BF16),
             pltpu.VMEM((3, 4, 16, 1152), BF16),
             pltpu.VMEM((3, 4, 16, 1152), BF16),
@@ -858,7 +876,7 @@
         out_shape=(*shapes, row, row, row),
         in_specs=[vmem] * 4,
         out_specs=(hbm,) * 6,
-        scratch_shapes=[dma((6,))],
+        scratch_shapes=[dma((9,))],
         cost_estimate=pl.CostEstimate(flops=0, bytes_accessed=3500000, transcendentals=0),
     )(*(pltpu.with_memory_space_constraint(a, pltpu.VMEM) for a in (up, lg, kg, small)))
     return up, lg, kg, bias_grad[0], gain_grad[0], shift_grad[0]

time: 43.9 us -> 42.8 us (0.975)
  Pallas kernels: 43.2 us -> 42.1 us
    pallas_call x1, Pallas kernels: 41.3 us -> 40.3 us  [local(): pl.pallas_call(functools.partial(body, float(count)), out_shape=(*shapes,...]
where the time goes in v2:
time: 42.8 us; the launch traced here: 42.7 us
  Pallas kernels  42.1 us (98%)
  between operations  0.64 us (1%)
    pallas_call x1, Pallas kernels, local(): pl.pallas_call(functools.partial(body, float(count)), out_shape=(*shapes,...  40.3 us
    pallas_call x1, Pallas kernels, local(): pl.pallas_call(emit, out_shape=(*shapes, row, row, row), in_specs=[vmem]...  1.83 us

profile of v2, /device:TPU:1, one launch (start us, length us, event | category | flops | bytes accessed | tf_op | source)
XLA Modules:
  0.0 42.7 jit_solution(3894049171404922183)
XLA Ops:
  0.6 40.3 %shard_map.109 = (bf16[1,2,8,320,128]{4,3,2,1,0:T(8,128)(2,1)S(1)}, bf16[1,2,4,160,128]{4,3,2,1,0:T(8,128)(2,1)S(1)}, f32[3,3,384,128]{3,2,1,0:T(8,128)S(1)}, f32[8,128]{1,0:T(8,128)S(1)}) custom-call(bf16[1,2,4,160,128]{4,3,2,1,0:T(8,128)(2,1)} %lat_hbm.1, bf16[1,2,8,320,128]{4,3,2,1,0:T(8,128)(2,1)} %cot_hbm.1, f32[1,128]{1,0:T(1,128)} %bitcast.6, ...), custom_call_target="tpu_custom_call" | custom-call | flops 3397386240 | bytes 6000000 | tf_op jit(solution)/shard_map/pallas_call | solution.py:824
  40.9 1.8 %shard_map.110 = (bf16[1,2,8,320,128]{4,3,2,1,0:T(8,128)(2,1)}, bf16[1,2,4,160,128]{4,3,2,1,0:T(8,128)(2,1)}, f32[3,3,384,128]{3,2,1,0:T(8,128)}, f32[1,128]{1,0...) custom-call(bf16[1,2,8,320,128]{4,3,2,1,0:T(8,128)(2,1)S(1)} %get-tuple-element.16.up, ...), custom_call_target="tpu_custom_call" | custom-call | bytes 3500000 | tf_op jit(solution)/shard_map/pallas_call | solution.py:874

commit v3 on v2

--- a/solution.py
+++ b/solution.py
@@ -421,12 +421,13 @@
     }
 
     exchange_wait(stat_z)
-    lane_a = lax.broadcasted_iota(jnp.int32, (128, 128), 0) >> 2
-    lane_b = lax.broadcasted_iota(jnp.int32, (128, 128), 1) >> 2
-    same = jnp.where(lane_a == lane_b, 1.0, 0.0)
+    lane8 = lax.broadcasted_iota(jnp.int32, (8, 128), 1)
 
     def by_group(v):
-        return jnp.dot(v, same, precision=lax.Precision.HIGHEST, preferred_element_type=F32)
+        v = v + pltpu.roll(v, 127, 1)
+        v = jnp.where(lane8 % 4 == 0, v + pltpu.roll(v, 126, 1), 0.0)
+        v = v + pltpu.roll(v, 1, 1)
+        return v + pltpu.roll(v, 2, 1)
 
     sums = by_group(tile_sum(st2, "z")) / count
     mean = sums[0:1]
@@ -616,10 +617,12 @@
 
     def flip(n, carry):
         i, j = n // 3, n % 3
+        v = lax.dot_general(
+            eye, ker[i, j], (((1,), (1,)), ((), ())), preferred_element_type=F32
+        ).astype(BF16)
         for k in range(3):
-            kt[i, pl.ds(pl.multiple_of(j * 384 + k * 128, 128), 128), :] = ker[
-                i, j, k * 128 : (k + 1) * 128, :
-            ].T
+            rows = pl.ds(pl.multiple_of(j * 384 + k * 128, 128), 128)
+            kt[i, rows, :] = v[:, k * 128 : (k + 1) * 128]
         return carry
 
     lax.fori_loop(0, 9, flip, 0)

time: 42.8 us -> 43.8 us (1.023)
  Pallas kernels: 42.1 us -> 43 us
    pallas_call x1, Pallas kernels: 40.3 us -> 41.2 us  [local(): pl.pallas_call(functools.partial(body, float(count)), out_shape=(*shapes,...]
where the time goes in v3:
time: 43.8 us; the launch traced here: 43.7 us
  Pallas kernels  43 us (98%)
  between operations  0.64 us (1%)
    pallas_call x1, Pallas kernels, local(): pl.pallas_call(functools.partial(body, float(count)), out_shape=(*shapes,...  41.2 us
    pallas_call x1, Pallas kernels, local(): pl.pallas_call(emit, out_shape=(*shapes, row, row, row), in_specs=[vmem]...  1.83 us

profile of v3, /device:TPU:1, one launch (start us, length us, event | category | flops | bytes accessed | tf_op | source)
XLA Modules:
  0.0 43.7 jit_solution(1227694804505027434)
XLA Ops:
  0.6 41.2 %shard_map.109 = (bf16[1,2,8,320,128]{4,3,2,1,0:T(8,128)(2,1)S(1)}, bf16[1,2,4,160,128]{4,3,2,1,0:T(8,128)(2,1)S(1)}, f32[3,3,384,128]{3,2,1,0:T(8,128)S(1)}, f32[8,128]{1,0:T(8,128)S(1)}) custom-call(bf16[1,2,4,160,128]{4,3,2,1,0:T(8,128)(2,1)} %lat_hbm.1, bf16[1,2,8,320,128]{4,3,2,1,0:T(8,128)(2,1)} %cot_hbm.1, f32[1,128]{1,0:T(1,128)} %bitcast.6, ...), custom_call_target="tpu_custom_call" | custom-call | flops 3397386240 | bytes 6000000 | tf_op jit(solution)/shard_map/pallas_call | solution.py:827
  41.9 1.8 %shard_map.110 = (bf16[1,2,8,320,128]{4,3,2,1,0:T(8,128)(2,1)}, bf16[1,2,4,160,128]{4,3,2,1,0:T(8,128)(2,1)}, f32[3,3,384,128]{3,2,1,0:T(8,128)}, f32[1,128]{1,0...) custom-call(bf16[1,2,8,320,128]{4,3,2,1,0:T(8,128)(2,1)S(1)} %get-tuple-element.16.up, ...), custom_call_target="tpu_custom_call" | custom-call | bytes 3500000 | tf_op jit(solution)/shard_map/pallas_call | solution.py:877

commit v4 on v3

--- a/solution.py
+++ b/solution.py
@@ -12,7 +12,7 @@
 F32 = jnp.float32
 BF16 = jnp.bfloat16
 
-ORDER = {2: ("x", "y", "z"), 1: ("y", "z", "x"), 0: ("z", "x", "y")}
+ORDER = {2: ("z", "x", "y"), 1: ("x", "y", "z"), 0: ("y", "z", "x")}
 
 
 def body(
@@ -103,14 +103,15 @@
         pltpu.make_async_copy(bias_hbm, vec.at[1:2], lsem.at[5]),
         pltpu.make_async_copy(kbias_hbm, vec.at[2:3], lsem.at[6]),
     ]
-    for c in loads:
-        c.start()
+    loads[0].start()
 
     barrier = pltpu.get_barrier_semaphore()
     greeted = [peer("h", d) for d in range(1, 8)]
     greeted += [peer("z", d) for d in range(1, 4)] + [peer("y", d) for d in range(1, 4)]
     for to in greeted:
         pl.semaphore_signal(barrier, inc=1, device_id=to, device_id_type=MESH)
+    for c in loads[1:]:
+        c.start()
 
     row16 = lax.broadcasted_iota(jnp.int32, (16, 128), 0)
 
@@ -160,6 +161,11 @@
 
     st1[h] = rows_of(s_sum, q_sum)
 
+    loads[1].wait()
+    bias_total = pool_frame(0, zero8)
+    loads[2].wait()
+    bias_total = pool_frame(1, bias_total)
+
     pl.semaphore_wait(barrier, 13)
 
     def exchange_start(buf, axis, base):
@@ -236,9 +242,6 @@
         def _(down=down):
             lat_row(2, down).start()
 
-    loads[1].wait()
-    bias_total = pool_frame(0, zero8)
-
     @pl.when(has_prev)
     def _():
         for part in range(3):
@@ -249,9 +252,6 @@
         @pl.when(there)
         def _(down=down):
             dc_row(0, down).start()
-
-    loads[2].wait()
-    bias_total = pool_frame(1, bias_total)
 
     for down, there in ((0, has_up), (1, has_down)):
 
@@ -375,6 +375,18 @@
 
         lax.fori_loop(0, 2, outer, 0)
         special_rows(4 + t)
+
+    loads[3].wait()
+
+    def flip(n, carry):
+        i, j = n // 3, n % 3
+        for k in range(3):
+            kt[i, pl.ds(pl.multiple_of(j * 384 + k * 128, 128), 128), :] = ker[
+                i, j, k * 128 : (k + 1) * 128, :
+            ].T
+        return carry
+
+    lax.fori_loop(0, 9, flip, 0)
 
     forward(0)
     ahead_inner(0)
@@ -487,18 +499,27 @@
         pre = normed(f, r) * gain + shift
         act_line(f, r, pre / (1.0 + jnp.exp(-pre)))
 
+    def own_lines_of(p, i):
+        return dslab[pl.ds(slot_of[p, i], 1), 1:5].reshape(640, 384)
+
     def weight_grad(i):
+        if i == 0:
+            left = actt[:, :, 640:1280].reshape(384, 640)
+            right = own_lines_of(0, 0)
+            past = jnp.dot(
+                pastt[...],
+                jnp.concatenate([taken(3, j) for j in range(3)], axis=1),
+                preferred_element_type=F32,
+            )
+        else:
+            left = actt[...].reshape(384, 1280)
+            right = jnp.concatenate([own_lines_of(1, i), own_lines_of(0, i)], axis=0)
+        part = jnp.dot(left, right, preferred_element_type=F32)
         for j in range(3):
-            mine = dslab[pl.ds(slot_of[0, i], 1), 1:5].reshape(640, 384)
+            v = part[j * 128 : (j + 1) * 128]
             if i == 0:
-                right = jnp.concatenate([mine, taken(3, j)], axis=0)
-                left = jnp.concatenate([actt[j, :, 640:1280], pastt[...]], axis=1)
-            else:
-                other = dslab[slot_of[1, i], 1:5].reshape(640, 384)
-                right = jnp.concatenate([other, mine], axis=0)
-                left = actt[j]
-            part = jnp.dot(left, right, preferred_element_type=F32)
-            g[i, :, :, j * 384 : (j + 1) * 384] = part.reshape(8, 16, 384)
+                v = v + past[:, j * 384 : (j + 1) * 384]
+            g[i, :, :, j * 384 : (j + 1) * 384] = v.reshape(8, 16, 384)
 
     copies = {}
 
@@ -612,20 +633,6 @@
             def _(down=down):
                 lat_row(0, down).start()
 
-
-    loads[3].wait()
-
-    def flip(n, carry):
-        i, j = n // 3, n % 3
-        v = lax.dot_general(
-            eye, ker[i, j], (((1,), (1,)), ((), ())), preferred_element_type=F32
-        ).astype(BF16)
-        for k in range(3):
-            rows = pl.ds(pl.multiple_of(j * 384 + k * 128, 128), 128)
-            kt[i, rows, :] = v[:, k * 128 : (k + 1) * 128]
-        return carry
-
-    lax.fori_loop(0, 9, flip, 0)
 
     reduce_1(0)
 

time: 43.8 us -> 42.4 us (0.968)
  Pallas kernels: 43 us -> 41.6 us
    pallas_call x1, Pallas kernels: 41.2 us -> 39.8 us  [local(): pl.pallas_call(functools.partial(body, float(count)), out_shape=(*shapes,...]
where the time goes in v4:
time: 42.4 us; the launch traced here: 42.2 us
  Pallas kernels  41.6 us (98%)
  between operations  0.64 us (2%)
    pallas_call x1, Pallas kernels, local(): pl.pallas_call(functools.partial(body, float(count)), out_shape=(*shapes,...  39.8 us
    pallas_call x1, Pallas kernels, local(): pl.pallas_call(emit, out_shape=(*shapes, row, row, row), in_specs=[vmem]...  1.83 us

profile of v4, /device:TPU:1, one launch (start us, length us, event | category | flops | bytes accessed | tf_op | source)
XLA Modules:
  0.0 42.2 jit_solution(8707772019868853873)
XLA Ops:
  0.6 39.8 %shard_map.109 = (bf16[1,2,8,320,128]{4,3,2,1,0:T(8,128)(2,1)S(1)}, bf16[1,2,4,160,128]{4,3,2,1,0:T(8,128)(2,1)S(1)}, f32[3,3,384,128]{3,2,1,0:T(8,128)S(1)}, f32[8,128]{1,0:T(8,128)S(1)}) custom-call(bf16[1,2,4,160,128]{4,3,2,1,0:T(8,128)(2,1)} %lat_hbm.1, bf16[1,2,8,320,128]{4,3,2,1,0:T(8,128)(2,1)} %cot_hbm.1, f32[1,128]{1,0:T(1,128)} %bitcast.6, ...), custom_call_target="tpu_custom_call" | custom-call | flops 3397386240 | bytes 6000000 | tf_op jit(solution)/shard_map/pallas_call | solution.py:834
  40.4 1.8 %shard_map.110 = (bf16[1,2,8,320,128]{4,3,2,1,0:T(8,128)(2,1)}, bf16[1,2,4,160,128]{4,3,2,1,0:T(8,128)(2,1)}, f32[3,3,384,128]{3,2,1,0:T(8,128)}, f32[1,128]{1,0...) custom-call(bf16[1,2,8,320,128]{4,3,2,1,0:T(8,128)(2,1)S(1)} %get-tuple-element.16.up, ...), custom_call_target="tpu_custom_call" | custom-call | bytes 3500000 | tf_op jit(solution)/shard_map/pallas_call | solution.py:884

commit v5 on v4

--- a/solution.py
+++ b/solution.py
@@ -588,21 +588,30 @@
         me = core * 4 + place[axis]
         fin[i, me] = total_of(e3, i)
         copies[i, 4] = []
+        copies[i, 5] = []
         for d in range(1, 4):
             n = 9 + d
             c = remote(fin.at[i, me], fin.at[i, me], ar_ss.at[i, n], ar_rs.at[i, n], peer(axis, d))
             c.start()
             copies[i, 4].append(c)
-
-    def gather_c(i):
-        for c in copies[i, 4]:
-            c.wait_recv()
-        half = pl.ds(core * 4, 4)
+        to_core(i, me, 0)
+
+    def to_core(i, block, d):
         c = remote(
-            fin.at[i, half], fin.at[i, half], ar_ss.at[i, 13], ar_rs.at[i, 13], peer("core", 0)
+            fin.at[i, block],
+            fin.at[i, block],
+            ar_ss.at[i, 13 + d],
+            ar_rs.at[i, 13 + d],
+            peer("core", 0),
         )
         c.start()
-        copies[i, 5] = [c]
+        copies[i, 5].append(c)
+
+    def gather_c(i):
+        here = place[ORDER[i][0]]
+        for d in (3, 1, 2):
+            copies[i, 4][d - 1].wait_recv()
+            to_core(i, core * 4 + lax.rem(here - d + 4, 4), d)
 
     def finish(i):
         for c in copies[i, 5]:
@@ -872,8 +881,8 @@
             dma((14,)),
             dma((28,)),
             dma((28,)),
-            dma((3, 14)),
-            dma((3, 14)),
+            dma((3, 17)),
+            dma((3, 17)),
         ],
         compiler_params=pltpu.CompilerParams(
             collective_id=0, has_side_effects=True, vmem_limit_bytes=40 * 1024 * 1024

time: 42.4 us -> 42.3 us (level)
  no operation moved by 1% of the time
where the time goes in v5:
time: 42.3 us; the launch traced here: 42.2 us
  Pallas kernels  41.6 us (98%)
  between operations  0.64 us (2%)
    pallas_call x1, Pallas kernels, local(): pl.pallas_call(functools.partial(body, float(count)), out_shape=(*shapes,...  39.7 us
    pallas_call x1, Pallas kernels, local(): pl.pallas_call(emit, out_shape=(*shapes, row, row, row), in_specs=[vmem]...  1.83 us

profile of v5, /device:TPU:1, one launch (start us, length us, event | category | flops | bytes accessed | tf_op | source)
XLA Modules:
  0.0 42.2 jit_solution(17366757897545812585)
XLA Ops:
  0.6 39.7 %shard_map.109 = (bf16[1,2,8,320,128]{4,3,2,1,0:T(8,128)(2,1)S(1)}, bf16[1,2,4,160,128]{4,3,2,1,0:T(8,128)(2,1)S(1)}, f32[3,3,384,128]{3,2,1,0:T(8,128)S(1)}, f32[8,128]{1,0:T(8,128)S(1)}) custom-call(bf16[1,2,4,160,128]{4,3,2,1,0:T(8,128)(2,1)} %lat_hbm.1, bf16[1,2,8,320,128]{4,3,2,1,0:T(8,128)(2,1)} %cot_hbm.1, f32[1,128]{1,0:T(1,128)} %bitcast.6, ...), custom_call_target="tpu_custom_call" | custom-call | flops 3397386240 | bytes 6000000 | tf_op jit(solution)/shard_map/pallas_call | solution.py:843
  40.4 1.8 %shard_map.110 = (bf16[1,2,8,320,128]{4,3,2,1,0:T(8,128)(2,1)}, bf16[1,2,4,160,128]{4,3,2,1,0:T(8,128)(2,1)}, f32[3,3,384,128]{3,2,1,0:T(8,128)}, f32[1,128]{1,0...) custom-call(bf16[1,2,8,320,128]{4,3,2,1,0:T(8,128)(2,1)S(1)} %get-tuple-element.16.up, ...), custom_call_target="tpu_custom_call" | custom-call | bytes 3500000 | tf_op jit(solution)/shard_map/pallas_call | solution.py:893
